TPU v7x, 32 devices: a whole 2x2x4 slice. The times are simulated.
32 devices in a mesh: groups: 2 (over y), tile: 4 (over z), dp: 2 (over x), chan: 2 (over core).
Axes of the slice: x: 2, y: 2, z: 4, core: 2. Of those that a mesh axis runs over, the one named last changes fastest.
Arguments:
- activations: bfloat16 [8, 64, 32, 256], P(('groups', 'dp'), 'chan', 'tile'), parts along dimension 0, may hold values from -6 to 6
- occupancy: int32 [8, 4, 2, 2], P(('groups', 'dp'), 'tile'), parts along dimension 0, may hold values 0 or 1
- weight: bfloat16 [27, 64, 64], replicated, may hold values from -0.15625 to 0.15625
- cotangent: bfloat16 [8, 64, 32, 256], P(('groups', 'dp'), 'chan', 'tile'), parts along dimension 0, may hold values from -6 to 6
Outputs:
- output: bfloat16 [8, 64, 32, 256], P(('groups', 'dp'), 'chan', 'tile'), parts along dimension 0
- input_grad: bfloat16 [8, 64, 32, 256], P(('groups', 'dp'), 'chan', 'tile'), parts along dimension 0
- weight_grad: float32 [54, 64, 64], P('groups', 'chan'), parts along dimension 0
There are 2 independent parts, one for each index of `groups`. A program takes and returns all parts, laid end to end along the dimension named above; an argument that names none is the same for every part. Nothing has to cross between parts.
Inputs may be any that keep to these rules, and one draw needn't show every extreme that they name: `occupancy`: 1 marks a tile that holds tissue, 0 an empty one.
All inputs are finite; a program needn't handle non-finite values. No bound on the sum of `occupancy` on one device may be relied on, other than what follows from the above.
Results may differ from a plain program's by a relative error of at most 0.003.
Values may be sent and summed in bfloat16 or wider, within the bound.
A program may use at most 64 MiB of HBM per device.

v0:
```python
import math

import jax
import jax.numpy as jnp
from jax import lax
from jax.sharding import PartitionSpec as P

E = 8
GX = 2
GY = 2


def with_halo(cells, sides, width):
    for axis, dim in sides:
        count = lax.axis_size(axis)
        ends = count - 1
        head = lax.slice_in_dim(cells, 0, width, axis=dim)
        tail = lax.slice_in_dim(cells, cells.shape[dim] - width, cells.shape[dim], axis=dim)
        cells = jnp.concatenate(
            [
                lax.ppermute(tail, axis, [(i, (i + 1) % count) for i in range(ends)]),
                cells,
                lax.ppermute(head, axis, [((i + 1) % count, i) for i in range(ends)]),
            ],
            axis=dim,
        )
    return cells


def voxel_live(occupancy):
    batches, layers, tiles_x, tiles_y = occupancy.shape
    spread = jnp.broadcast_to(
        occupancy[:, :, None, :, None, :, None], (batches, layers, E, tiles_x, E, tiles_y, E)
    )
    return spread.reshape(batches, 1, layers * E, tiles_x * E * tiles_y * E)


def flat_padded(full):
    batches, channels, depth_rim, plane_size = full.shape
    width_y = GY * E
    flat = full.reshape(batches, channels, depth_rim * plane_size)
    return jnp.pad(flat, ((0, 0), (0, 0), (width_y + 1, width_y + 1)))


def shifted(padded, along_z, step_x, step_y, inner_len, plane_size):
    width_y = GY * E
    start = along_z * plane_size + (width_y + 1) + step_x * width_y + step_y
    return lax.slice_in_dim(padded, start, start + inner_len, axis=2)


def edge_mask(step_x, step_y, depth, plane_size):
    width_y = GY * E
    width_x = GX * E
    place = jnp.arange(plane_size, dtype=jnp.int32)
    row_x = place // width_y + step_x
    row_y = place % width_y + step_y
    valid = (row_x >= 0) & (row_x < width_x) & (row_y >= 0) & (row_y < width_y)
    return jnp.tile(valid.astype(jnp.float32), depth)


def shards(activations, occupancy, weight, cotangent):
    batches, own_channels, depth, plane_size = activations.shape
    inner_len = depth * plane_size
    own_start = lax.axis_index("chan") * own_channels
    weight_out = lax.dynamic_slice_in_dim(weight, own_start, own_channels, 1)
    weight_in = lax.dynamic_slice_in_dim(weight, own_start, own_channels, 2)
    live_mask = voxel_live(occupancy).astype(jnp.bfloat16)
    live_wide = live_mask.astype(jnp.float32)
    masked = activations * live_mask
    masked_rim = with_halo(masked, (("tile", 2),), 1)
    masked_full = lax.all_gather(masked_rim, "chan", axis=1, tiled=True)
    masked_flat = flat_padded(masked_full)
    summed = jnp.zeros((batches, own_channels, inner_len), jnp.float32)
    for plane_pos in range(9):
        along_x, along_y = (plane_pos // 3, plane_pos % 3)
        group_sum = jnp.zeros((batches, own_channels, inner_len), jnp.float32)
        for along_z in range(3):
            position = 9 * along_z + plane_pos
            source = shifted(masked_flat, along_z, along_x - 1, along_y - 1, inner_len, plane_size)
            group_sum = group_sum + jnp.einsum(
                "oi,siv->sov", weight_out[position], source, preferred_element_type=jnp.float32
            )
        summed = summed + edge_mask(along_x - 1, along_y - 1, depth, plane_size) * group_sum
    summed = summed.reshape(activations.shape)
    logistic = jax.nn.sigmoid(summed)
    output = (live_wide * (masked.astype(jnp.float32) + summed * logistic)).astype(jnp.bfloat16)
    slope = logistic * (1.0 + summed * (1.0 - logistic))
    grad_pre = (cotangent.astype(jnp.float32) * live_wide * slope).astype(jnp.bfloat16)
    grad_flat = grad_pre.reshape(batches, own_channels, inner_len)
    count = batches * lax.axis_size("dp") * depth * lax.axis_size("tile") * plane_size
    scale_factor = 1.0 / math.sqrt(count)
    grad_rim = with_halo(grad_pre, (("tile", 2),), 1)
    grad_full = lax.all_gather(grad_rim, "chan", axis=1, tiled=True)
    grad_padded = flat_padded(grad_full)
    back = jnp.zeros((batches, own_channels, inner_len), jnp.float32)
    for input_plane_pos in range(9):
        input_along_x, input_along_y = (input_plane_pos // 3, input_plane_pos % 3)
        group_sum = jnp.zeros((batches, own_channels, inner_len), jnp.float32)
        for input_along_z in range(3):
            input_position = 9 * input_along_z + input_plane_pos
            input_source = shifted(
                grad_padded,
                2 - input_along_z,
                1 - input_along_x,
                1 - input_along_y,
                inner_len,
                plane_size,
            )
            group_sum = group_sum + jnp.einsum(
                "oi,sov->siv",
                weight_in[input_position],
                input_source,
                preferred_element_type=jnp.float32,
            )
        back = back + edge_mask(1 - input_along_x, 1 - input_along_y, depth, plane_size) * group_sum
    back = back.reshape(activations.shape)
    input_grad = (live_wide * (cotangent.astype(jnp.float32) + back)).astype(jnp.bfloat16)
    pieces = [None] * 27
    for plane_pos in range(9):
        along_x, along_y = (plane_pos // 3, plane_pos % 3)
        border = edge_mask(along_x - 1, along_y - 1, depth, plane_size).astype(jnp.bfloat16)
        grad_edge = grad_flat * border
        for along_z in range(3):
            position = 9 * along_z + plane_pos
            source = shifted(masked_flat, along_z, along_x - 1, along_y - 1, inner_len, plane_size)
            pieces[position] = jnp.einsum(
                "sov,siv->oi", grad_edge, source, preferred_element_type=jnp.float32
            )
    local_term = jnp.stack(pieces)
    weight_grad = lax.psum(local_term, ("tile", "dp")) * scale_factor
    return (output, input_grad, weight_grad)


def solution(mesh):
    return jax.shard_map(
        shards,
        mesh=mesh,
        in_specs=(
            P(("groups", "dp"), "chan", "tile", None),
            P(("groups", "dp"), "tile", None, None),
            P(),
            P(("groups", "dp"), "chan", "tile", None),
        ),
        out_specs=(
            P(("groups", "dp"), "chan", "tile", None),
            P(("groups", "dp"), "chan", "tile", None),
            P("groups", "chan", None),
        ),
        check_vma=False,
    )
```

profile of v0, /device:TPU:0, one launch (start us, length us, event | category | flops | bytes accessed | tf_op | source)
XLA Modules:
  0.0 131.8 jit_solution(1393877452400870475)
XLA Ops:
  7.2 0.7 convert_bitcast_fusion
  8.1 1.0 broadcast_multiply_fusion.1
  9.2 4.9 %collective-permute-start = (bf16[2,32,1,256]{3,2,1,0:T(2,128)(2,1)S(1)}, bf16[2,32,1,256]{3,2,1,0:T(2,128)(2,1)S(1)}, u32[]{:S(2)}, u32[]{:S(2)}) collective-permute-start(bf16[2,32,1,256]{3,2,1,0:T(2,128)(2,1)S(1)} %get-tuple-element.7), channel_id=1, source_target_pairs={{0,4},{4,8},{8,12},{1,5},{5,9},{9,13},{2,6},{6,10},{10,14},{3,7},{... | collective-permute-start | bytes 98312 | tf_op jit(solution)/shard_map/ppermute | solution.py:21
  14.2 1.3 collective-permute-start.1
  16.0 4.3 %collective-permute-done.1 = bf16[2,32,1,256]{3,2,1,0:T(2,128)(2,1)S(1)} collective-permute-done((bf16[2,32,1,256]{3,2,1,0:T(2,128)(2,1)S(1)}, bf16[2,32,1,256]{3,2,1,0:T(2,128)(2,1)S(1)}, u32[]{:S(2)}, u32[]{:S(2)}) %collective-permute-start.1) | collective-permute-done | bytes 32800 | tf_op jit(solution)/shard_map/ppermute | solution.py:23
  20.6 2.6 %all_gather.6 = bf16[2,64,10,256]{3,2,1,0:T(8,128)(2,1)S(1)} all-gather(bf16[2,32,10,256]{3,2,1,0:T(8,128)(2,1)S(1)} %pad_maximum_fusion), channel_id=1, replica_groups=mesh['groups'=2,'tile'=4,'dp'=2,'chan'=2] {'chan'}, dimensions={1}, use_global_device_ids=true | all-gather | bytes 983040 | tf_op jit(solution)/shard_map/all_gather | solution.py:71
  23.2 0.4 reshape.170
  32.6 0.8 copy-done.1
  33.4 1.0 fusion.62
  36.3 0.4 fusion.55
  36.7 0.4 fusion.54
  37.8 0.4 fusion.51
  38.5 0.4 fusion.49
  39.5 0.4 fusion.46
  41.8 0.4 fusion.40
  43.8 3.5 %collective-permute-start.2 = (bf16[2,32,1,256]{3,2,1,0:T(2,128)(2,1)S(1)}, bf16[2,32,1,256]{3,2,1,0:T(2,128)(2,1)S(1)}, u32[]{:S(2)}, u32[]{:S(2)}) collective-permute-start(bf16[2,32,1,256]{3,2,1,0:T(2,128)(2,1)S(1)} %get-tuple-element.5), channel_id=1, source_target_pairs={{0,4},{4,8},{8,12},{1,5},{5,9},{9,13},{2,6},{6,10},{10,14},{3,7},{... | collective-permute-start | bytes 98312 | tf_op jit(solution)/shard_map/ppermute | solution.py:21
  47.3 1.3 collective-permute-start.3
  49.0 0.8 copy-done.3
  49.8 3.7 %collective-permute-done.3 = bf16[2,32,1,256]{3,2,1,0:T(2,128)(2,1)S(1)} collective-permute-done((bf16[2,32,1,256]{3,2,1,0:T(2,128)(2,1)S(1)}, bf16[2,32,1,256]{3,2,1,0:T(2,128)(2,1)S(1)}, u32[]{:S(2)}, u32[]{:S(2)}) %collective-permute-start.3) | collective-permute-done | bytes 32800 | tf_op jit(solution)/shard_map/ppermute | solution.py:23
  53.8 2.6 %all_gather.7 = bf16[2,64,10,256]{3,2,1,0:T(8,128)(2,1)S(1)} all-gather(bf16[2,32,10,256]{3,2,1,0:T(8,128)(2,1)S(1)} %pad_maximum_fusion.1), channel_id=1, replica_groups=mesh['groups'=2,'tile'=4,'dp'=2,'chan'=2] {'chan'}, dimensions={1}, use_global_device_ids=true | all-gather | bytes 983040 | tf_op jit(solution)/shard_map/all_gather | solution.py:93
  56.4 0.4 reshape.172
  56.8 0.4 fusion.80
  57.2 0.4 fusion.107
  57.5 0.4 fusion.105
  57.9 0.4 fusion.103
  58.3 0.4 fusion.101
  59.0 0.4 fusion.83
  59.4 0.4 fusion.77
  59.7 0.4 fusion.74
  60.1 0.4 convolution_add_fusion.5
  60.5 0.4 convolution_add_fusion.17
  60.9 0.4 convolution_add_fusion.15
  61.3 0.4 fusion.7
  61.6 0.4 convolution_add_fusion.13
  62.0 0.4 fusion.6
  62.4 0.4 convolution_add_fusion.11
  62.8 0.4 fusion.5
  63.8 0.4 convolution_add_fusion.7
  64.2 0.4 fusion.3
  64.6 0.4 convolution_add_fusion.3
  65.0 0.4 fusion.1
  65.4 0.4 convolution_add_fusion.1
  65.7 0.4 fusion
  66.1 0.4 fusion.30
  66.6 0.4 fusion.33
  67.1 0.8 fusion.64
  67.9 55.2 %all-reduce.4.cloned.1.call-done = f32[27,32,64]{2,1,0:T(8,128)} async-done(((f32[27,32,64]{2,1,0:T(8,128)}), f32[27,32,64]{2,1,0:T(8,128)}) %all-reduce.4.cloned.1.call-update) | async-done | bytes 221200 | tf_op jit(solution)/shard_map/psum | solution.py:130
  123.1 1.8 %broadcast_multiply_fusion = f32[27,32,64]{2,1,0:T(8,128)} fusion(f32[27,32,64]{2,1,0:T(8,128)} %all-reduce.4.cloned.1.call-done), kind=kLoop, calls=%fused_computation.250 | loop fusion | flops 55296 | bytes 442368 | tf_op jit(solution)/shard_map/mul | solution.py:130
  (103 shorter events, 18.9 us)
Async XLA Ops:
  7.2 16.4 %copy-start = (bf16[27,64,64]{2,1,0:T(8,128)(2,1)S(1)}, bf16[27,64,64]{2,1,0:T(8,128)(2,1)}, u32[]{:S(2)}) copy-start(bf16[27,64,64]{2,1,0:T(8,128)(2,1)} %param.6) | copy-start | bytes 663556
  7.2 116.0 %all-reduce.4.cloned.1.call-start = ((), (), s32[]{:S(2)}) async-start(), calls=%async_computation | async-start | bytes 884736 | tf_op jit(solution)/shard_map/psum | solution.py:130
  9.2 6.8 %collective-permute-start = (bf16[2,32,1,256]{3,2,1,0:T(2,128)(2,1)S(1)}, bf16[2,32,1,256]{3,2,1,0:T(2,128)(2,1)S(1)}, u32[]{:S(2)}, u32[]{:S(2)}) collective-permute-start(bf16[2,32,1,256]{3,2,1,0:T(2,128)(2,1)S(1)} %get-tuple-element.7), channel_id=1, source_target_pairs={{0,4},{4,8},{8,12},{1,5},{5,9},{9,13},{2,6},{6,10},{10,14},{3,7},{... | collective-permute-start | bytes 98312 | tf_op jit(solution)/shard_map/ppermute | solution.py:21
  14.2 6.2 %collective-permute-start.1 = (bf16[2,32,1,256]{3,2,1,0:T(2,128)(2,1)S(1)}, bf16[2,32,1,256]{3,2,1,0:T(2,128)(2,1)S(1)}, u32[]{:S(2)}, u32[]{:S(2)}) collective-permute-start(bf16[2,32,1,256]{3,2,1,0:T(2,128)(2,1)S(1)} %get-tuple-element.8), channel_id=1, source_target_pairs={{4,0},{8,4},{12,8},{5,1},{9,5},{13,9},{6,2},{10,6},{14,10},{7,3},{... | collective-permute-start | bytes 98312 | tf_op jit(solution)/shard_map/ppermute | solution.py:23
  32.4 1.0 copy-start.1
  32.4 1.0 copy-start.2
  43.8 5.9 %collective-permute-start.2 = (bf16[2,32,1,256]{3,2,1,0:T(2,128)(2,1)S(1)}, bf16[2,32,1,256]{3,2,1,0:T(2,128)(2,1)S(1)}, u32[]{:S(2)}, u32[]{:S(2)}) collective-permute-start(bf16[2,32,1,256]{3,2,1,0:T(2,128)(2,1)S(1)} %get-tuple-element.5), channel_id=1, source_target_pairs={{0,4},{4,8},{8,12},{1,5},{5,9},{9,13},{2,6},{6,10},{10,14},{3,7},{... | collective-permute-start | bytes 98312 | tf_op jit(solution)/shard_map/ppermute | solution.py:21
  47.3 6.2 %collective-permute-start.3 = (bf16[2,32,1,256]{3,2,1,0:T(2,128)(2,1)S(1)}, bf16[2,32,1,256]{3,2,1,0:T(2,128)(2,1)S(1)}, u32[]{:S(2)}, u32[]{:S(2)}) collective-permute-start(bf16[2,32,1,256]{3,2,1,0:T(2,128)(2,1)S(1)} %get-tuple-element.6), channel_id=1, source_target_pairs={{4,0},{8,4},{12,8},{5,1},{9,5},{13,9},{6,2},{10,6},{14,10},{7,3},{... | collective-permute-start | bytes 98312 | tf_op jit(solution)/shard_map/ppermute | solution.py:23
  49.0 0.8 copy-start.3
Sparse Core Ops, SparseCore 0:
  49.9 73.1 all-reduce.3
where the time goes:
time: 132 us
  waiting for transfers between devices  63.4 us (48%)
  matrix products  28.2 us (21%)
  between operations  14.7 us (11%)
  starting transfers between devices  11 us (8%)
  other arithmetic  6.03 us (5%)
  blocking collectives  5.11 us (4%)
  local copies, waits for them, and re-layouts  3.32 us (3%)
    psum x1, waiting for transfers between devices, shards(): weight_grad = lax.psum(local_term, ('tile', 'dp')) * scale_factor  55.2 us
    dot_general x27, matrix products, shards(): jnp.einsum('oi,sov->siv', weight_in[input_position], input_source, prefer...  9.99 us
    dot_general x27, matrix products, shards(): jnp.einsum('sov,siv->oi', grad_edge, source, preferred_element_type=jnp.f...  9.54 us
    dot_general x27, matrix products, shards(): jnp.einsum('oi,siv->sov', weight_out[position], source, preferred_element...  8.68 us
    ppermute x2, starting transfers between devices, with_halo(): lax.ppermute(tail, axis, [(i, (i + 1) % count) for i in range(ends)])  8.42 us
    ppermute x2, waiting for transfers between devices, with_halo(): lax.ppermute(head, axis, [((i + 1) % count, i) for i in range(ends)])  7.98 us
  transfers between devices with their start and end apart: 5, of which 4 were waited for; matrix products, arithmetic and copies ran while one was open for 9% of the time, Pallas kernels for 0%

commit v1 on v0

v1 whole, which is shorter than its diff:
```python
import functools
import math

import jax
import jax.numpy as jnp
from jax import lax
from jax.experimental import pallas as pl
from jax.experimental.pallas import tpu as pltpu
from jax.sharding import PartitionSpec as P

E = 8
GX = 2
GY = 2
WY = GY * E
PLANE = GX * E * WY
MESH = pl.DeviceIdType.MESH
BF16 = jnp.bfloat16
F32 = jnp.float32
ROWS = 16
TILES = 27


def dot(a, b):
    return lax.dot_general(a, b, (((1,), (0,)), ((), ())), preferred_element_type=F32)


def dot_nt(a, b):
    return lax.dot_general(a, b, (((1,), (1,)), ((), ())), preferred_element_type=F32)


def lanes(rows):
    return lax.broadcasted_iota(jnp.int32, (rows, PLANE), 1)


def kernel(
    tiles, dps, scale,
    act, cot, occ, w, out, grad_in, wg,
    x, xe, g, ge, gd, wf, wb, part, landed, total,
    xs, xr, gs, gr, rs, rr, ts, tr,
):
    batches, half, inner = act.shape
    depth = inner // PLANE
    me = {name: lax.axis_index(name) for name in ("tile", "dp", "chan")}
    t, c = me["tile"], me["chan"]
    other = 1 - c
    count = tiles * dps
    rank = t * dps + me["dp"]
    has_up = t < tiles - 1
    has_down = t > 0

    def member(j):
        r = lax.rem(rank + j, count)
        return r, {"tile": r // dps, "dp": lax.rem(r, dps)}

    barrier = pltpu.get_barrier_semaphore()

    def greet(device):
        pl.semaphore_signal(barrier, inc=1, device_id=device, device_id_type=MESH)

    greet({"chan": other})

    @pl.when(has_up)
    def _():
        greet({"tile": t + 1, "chan": other})

    @pl.when(has_down)
    def _():
        greet({"tile": t - 1, "chan": other})

    @pl.loop(1, count)
    def _(j):
        greet(member(j)[1])

    place = lanes(half)
    row = place // WY
    col = place % WY
    from_left = jnp.where(col > 0, 1.0, 0.0).astype(BF16)
    from_right = jnp.where(col < WY - 1, 1.0, 0.0).astype(BF16)
    has_above = row > 0
    has_below = row < GX * E - 1

    def live_of(b):
        def pick(i):
            return jnp.where(col < E, occ[b, 0, i, 0], occ[b, 0, i, 1])
        return jnp.where(row < E, pick(0), pick(1)).astype(F32)

    live = [live_of(b) for b in range(batches)]

    def spread(dst, b, q, ch, value, flip):
        first, last = (2, 0) if flip else (0, 2)
        dst[b, 3 * q + first, ch] = pltpu.roll(value, 1, 1) * from_left
        dst[b, 3 * q + 1, ch] = value
        dst[b, 3 * q + last, ch] = pltpu.roll(value, PLANE - 1, 1) * from_right

    def rim_zero(buf):
        zeros = jnp.zeros((half, PLANE), BF16)

        @pl.when(jnp.logical_not(has_down))
        def _():
            for b in range(batches):
                for ch in range(2):
                    buf[b, 0, ch] = zeros

        @pl.when(jnp.logical_not(has_up))
        def _():
            for b in range(batches):
                for ch in range(2):
                    buf[b, depth + 1, ch] = zeros

    def inside(buf, b, ch, send, recv):
        ref = buf.at[b, pl.ds(1, depth), ch]
        return pltpu.make_async_remote_copy(
            src_ref=ref, dst_ref=ref, send_sem=send.at[b, 0], recv_sem=recv.at[b, 0],
            device_id={"chan": other}, device_id_type=MESH,
        )

    def rim(buf, b, ch, up, to, send, recv):
        side = 1 if up else 3
        return pltpu.make_async_remote_copy(
            src_ref=buf.at[b, depth if up else 1, ch],
            dst_ref=buf.at[b, 0 if up else depth + 1, ch],
            send_sem=send.at[b, side + to], recv_sem=recv.at[b, side + ch],
            device_id={"tile": t + 1 if up else t - 1, "chan": to}, device_id_type=MESH,
        )

    def send_all(buf, b, send, recv):
        @pl.when(has_up)
        def _():
            for to in range(2):
                rim(buf, b, c, True, to, send, recv).start()

        @pl.when(has_down)
        def _():
            for to in range(2):
                rim(buf, b, c, False, to, send, recv).start()

        inside(buf, b, c, send, recv).start()

    def sent_all(buf, b, send, recv):
        @pl.when(has_up)
        def _():
            for to in range(2):
                rim(buf, b, c, True, to, send, recv).wait_send()

        @pl.when(has_down)
        def _():
            for to in range(2):
                rim(buf, b, c, False, to, send, recv).wait_send()

        inside(buf, b, c, send, recv).wait_send()

    def rims_arrive(buf, b, send, recv):
        @pl.when(has_down)
        def _():
            for ch in range(2):
                rim(buf, b, ch, True, 0, send, recv).wait_recv()

        @pl.when(has_up)
        def _():
            for ch in range(2):
                rim(buf, b, ch, False, 0, send, recv).wait_recv()

    def fill_rest(buf, dst, b, send, recv, flip):
        inside(buf, b, other, send, recv).wait_recv()
        for z in range(depth):
            spread(dst, b, z + 1, other, buf[b, z + 1, other], flip)
        rims_arrive(buf, b, send, recv)
        for q in (0, depth + 1):
            for ch in range(2):
                spread(dst, b, q, ch, buf[b, q, ch], flip)

    def conv(src, weight, b, z):
        wide = dot(weight[...], src[b, 3 * z:3 * z + 9].reshape(18 * half, PLANE))
        above = pltpu.roll(wide[:half], WY, 1)
        below = pltpu.roll(wide[2 * half:], PLANE - WY, 1)
        return wide[half:2 * half] + jnp.where(has_above, above, 0.0) + jnp.where(has_below, below, 0.0)

    rim_zero(x)
    rim_zero(g)
    for b in range(batches):
        mask = live[b].astype(BF16)
        for z in range(depth):
            x[b, z + 1, c] = act[b, :, z * PLANE:(z + 1) * PLANE] * mask

    pl.semaphore_wait(barrier, count + has_up.astype(jnp.int32) + has_down.astype(jnp.int32))
    for b in range(batches):
        send_all(x, b, xs, xr)

    for d in range(3):
        wf[d * half:(d + 1) * half] = jnp.concatenate(
            [w[9 * a + 3 * d + e, c] for a in range(3) for e in range(3)], axis=1
        )
    pick_own = (
        lax.broadcasted_iota(jnp.int32, (half, 2 * half), 1)
        == lax.broadcasted_iota(jnp.int32, (half, 2 * half), 0) + c * half
    )
    turned = dot_nt(
        jnp.where(pick_own, 1.0, 0.0).astype(BF16), w[...].reshape(54 * half, 2 * half)
    ).astype(BF16)
    for d in range(3):
        wb[d * half:(d + 1) * half] = jnp.concatenate(
            [
                turned[:, (9 * (2 - a) + 3 * (2 - d)) * 2 * half:(9 * (2 - a) + 3 * (2 - d) + 3) * 2 * half]
                for a in range(3)
            ],
            axis=1,
        )
    for b in range(batches):
        for z in range(depth):
            spread(xe, b, z + 1, c, x[b, z + 1, c], False)

    for b in range(batches):
        fill_rest(x, xe, b, xs, xr, False)
        for z in range(depth):
            pre = conv(xe, wf, b, z)
            s = 1.0 / (1.0 + jnp.exp(-pre))
            span = slice(z * PLANE, (z + 1) * PLANE)
            out[b, :, span] = (live[b] * (x[b, z + 1, c].astype(F32) + pre * s)).astype(BF16)
            slope = s * (1.0 + pre * (1.0 - s))
            own = (cot[b, :, span].astype(F32) * live[b] * slope).astype(BF16)
            g[b, z + 1, c] = own
        send_all(g, b, gs, gr)
        for z in range(depth):
            own = g[b, z + 1, c]
            spread(ge, b, z + 1, c, own, True)
            own = own.astype(F32)
            gd[b, z, 0] = jnp.where(has_below, pltpu.roll(own, PLANE - WY, 1), 0.0).astype(BF16)
            gd[b, z, 1] = g[b, z + 1, c]
            gd[b, z, 2] = jnp.where(has_above, pltpu.roll(own, WY, 1), 0.0).astype(BF16)

    per = part.shape[1] // ROWS
    for i in range(TILES, per * count):
        part[i // per, (i % per) * ROWS:(i % per + 1) * ROWS] = jnp.zeros((ROWS, 128), F32)
    for a in range(3):
        acc = None
        for b in range(batches):
            for z in range(depth):
                q = z + a
                one = dot_nt(
                    gd[b, z].reshape(3 * half, PLANE),
                    xe[b, 3 * q:3 * q + 3].reshape(6 * half, PLANE),
                )
                acc = one if acc is None else acc + one
        body = acc[:, :4 * half]
        rest = acc[:, 4 * half:]
        mid = 3 * half // 2
        body = jnp.concatenate(
            [body, jnp.concatenate([rest[:mid], rest[mid:]], axis=1)], axis=0
        )
        for h in range(9):
            i = 9 * a + h
            part[i // per, (i % per) * ROWS:(i % per + 1) * ROWS] = body[h * ROWS:(h + 1) * ROWS]

    def scatter(j):
        r, device = member(j)
        return pltpu.make_async_remote_copy(
            src_ref=part.at[r], dst_ref=landed.at[rank], send_sem=rs.at[r], recv_sem=rr.at[rank],
            device_id=device, device_id_type=MESH,
        )

    def scattered(j):
        r, device = member(j)
        return pltpu.make_async_remote_copy(
            src_ref=part.at[r], dst_ref=landed.at[r], send_sem=rs.at[r], recv_sem=rr.at[r],
            device_id=device, device_id_type=MESH,
        )

    def gather(j):
        r, device = member(j)
        return pltpu.make_async_remote_copy(
            src_ref=total.at[rank], dst_ref=total.at[rank], send_sem=ts.at[r], recv_sem=tr.at[rank],
            device_id=device, device_id_type=MESH,
        )

    def gathered(j):
        r, device = member(j)
        return pltpu.make_async_remote_copy(
            src_ref=total.at[r], dst_ref=total.at[r], send_sem=ts.at[r], recv_sem=tr.at[r],
            device_id=device, device_id_type=MESH,
        )

    @pl.loop(1, count)
    def _(j):
        scatter(j).start()

    landed[rank] = part[rank]

    def backward(b):
        fill_rest(g, ge, b, gs, gr, True)
        for z in range(depth):
            back = conv(ge, wb, b, z)
            span = slice(z * PLANE, (z + 1) * PLANE)
            grad_in[b, :, span] = (live[b] * (cot[b, :, span].astype(F32) + back)).astype(BF16)

    backward(0)

    @pl.loop(1, count)
    def _(j):
        scattered(j).wait_recv()

    summed = landed[0]
    for i in range(1, count):
        summed = summed + landed[i]
    total[rank] = (summed * scale).astype(BF16)

    @pl.loop(1, count)
    def _(j):
        gather(j).start()

    for b in range(1, batches):
        backward(b)

    for b in range(batches):
        sent_all(x, b, xs, xr)
        sent_all(g, b, gs, gr)

    @pl.loop(1, count)
    def _(j):
        scatter(j).wait_send()
        gather(j).wait_send()
        gathered(j).wait_recv()

    def tile(i):
        return total[i // per, (i % per) * ROWS:(i % per + 1) * ROWS].astype(F32)

    for a in range(3):
        for h in range(6):
            d, low = h // 2, (h % 2) * ROWS
            two = tile(9 * a + h)
            one = tile(9 * a + 6 + h % 3)
            k = 9 * a + 3 * d
            wg[k, low:low + ROWS] = two[:, :2 * half]
            wg[k + 1, low:low + ROWS] = two[:, 2 * half:]
            wg[k + 2, low:low + ROWS] = one[:, (h // 3) * 2 * half:(h // 3 + 1) * 2 * half]


def shards(tiles, dps, activations, occupancy, weight, cotangent):
    batches, half, depth, plane = activations.shape
    inner = depth * plane
    count = tiles * dps
    per = -(-TILES // count)
    scale = 1.0 / math.sqrt(batches * dps * depth * tiles * plane)
    act = activations.reshape(batches, half, inner)
    cot = cotangent.reshape(batches, half, inner)
    w = weight.reshape(27, 2, half, 2 * half)
    vmem = pl.BlockSpec(memory_space=pltpu.VMEM)
    out, grad_in, wg = pl.pallas_call(
        functools.partial(kernel, tiles, dps, scale),
        out_shape=(
            jax.ShapeDtypeStruct((batches, half, inner), BF16),
            jax.ShapeDtypeStruct((batches, half, inner), BF16),
            jax.ShapeDtypeStruct((27, half, 2 * half), F32),
        ),
        in_specs=[vmem, vmem, pl.BlockSpec(memory_space=pltpu.SMEM), vmem],
        out_specs=(vmem, vmem, vmem),
        scratch_shapes=[
            pltpu.VMEM((batches, depth + 2, 2, half, plane), BF16),
            pltpu.VMEM((batches, 3 * (depth + 2), 2, half, plane), BF16),
            pltpu.VMEM((batches, depth + 2, 2, half, plane), BF16),
            pltpu.VMEM((batches, 3 * (depth + 2), 2, half, plane), BF16),
            pltpu.VMEM((batches, depth, 3, half, plane), BF16),
            pltpu.VMEM((3 * half, 18 * half), BF16),
            pltpu.VMEM((3 * half, 18 * half), BF16),
            pltpu.VMEM((count, per * ROWS, 128), F32),
            pltpu.VMEM((count, per * ROWS, 128), F32),
            pltpu.VMEM((count, per * ROWS, 128), BF16),
            pltpu.SemaphoreType.DMA((batches, 5)),
            pltpu.SemaphoreType.DMA((batches, 5)),
            pltpu.SemaphoreType.DMA((batches, 5)),
            pltpu.SemaphoreType.DMA((batches, 5)),
            pltpu.SemaphoreType.DMA((count,)),
            pltpu.SemaphoreType.DMA((count,)),
            pltpu.SemaphoreType.DMA((count,)),
            pltpu.SemaphoreType.DMA((count,)),
        ],
        compiler_params=pltpu.CompilerParams(
            collective_id=0, has_side_effects=True, vmem_limit_bytes=40 * 1024 * 1024
        ),
        cost_estimate=pl.CostEstimate(flops=1400000000, bytes_accessed=2000000, transcendentals=131072),
    )(act, cot, occupancy, w)
    shape = (batches, half, depth, plane)
    return out.reshape(shape), grad_in.reshape(shape), wg


def solution(mesh):
    tiles, dps = mesh.shape["tile"], mesh.shape["dp"]
    return jax.shard_map(
        functools.partial(shards, tiles, dps),
        mesh=mesh,
        in_specs=(
            P(("groups", "dp"), "chan", "tile", None),
            P(("groups", "dp"), "tile", None, None),
            P(),
            P(("groups", "dp"), "chan", "tile", None),
        ),
        out_specs=(
            P(("groups", "dp"), "chan", "tile", None),
            P(("groups", "dp"), "chan", "tile", None),
            P("groups", "chan", None),
        ),
        check_vma=False,
    )
```

time: 132 us -> 31.8 us (0.24)
  waiting for transfers between devices: 63.4 us -> 0 us
  matrix products: 28.2 us -> 0 us
  Pallas kernels: 0 us -> 26.5 us
  between operations: 14.7 us -> 0.68 us
  starting transfers between devices: 11 us -> 0 us
  other arithmetic: 6.03 us -> 0 us
  blocking collectives: 5.11 us -> 0 us
    psum x1 -> x0, waiting for transfers between devices: 55.2 us -> none  [shards(): weight_grad = lax.psum(local_term, ('tile', 'dp')) * scale_factor]
    dot_general x81 -> x0, matrix products: 28.2 us -> none  [the longest x27 9.99 us: shards(): jnp.einsum('oi,sov->siv', weight_in[input_position], input_source, prefer...]
    pallas_call x0 -> x1, Pallas kernels: none -> 26.5 us  [shards(): pl.pallas_call(functools.partial(kernel, tiles, dps, scale), out_shape=(j...]
    ppermute x4 -> x0, starting transfers between devices: 11 us -> none  [the longest x2 8.42 us: with_halo(): lax.ppermute(tail, axis, [(i, (i + 1) % count) for i in range(ends)])]
    ppermute x4 -> x0, waiting for transfers between devices: 8.16 us -> none  [the longest x2 7.98 us: with_halo(): lax.ppermute(head, axis, [((i + 1) % count, i) for i in range(ends)])]
    all_gather x2 -> x0, blocking collectives: 5.11 us -> none  [the longest x1 2.56 us: shards(): masked_full = lax.all_gather(masked_rim, 'chan', axis=1, tiled=True)]
    mul x2 -> x0, other arithmetic: 2.79 us -> none  [the longest x1 1.82 us: shards(): weight_grad = lax.psum(local_term, ('tile', 'dp')) * scale_factor]
    convert_element_type x18 -> x0, other arithmetic: 2.59 us -> none  [the longest x1 1 us: shards(): (cotangent.astype(jnp.float32) * live_wide * slope).astype(jnp.bfloat16)]
  transfers between devices with their start and end apart: 5 -> 0, of which waited for: 4 -> 0; matrix products, arithmetic and copies ran while one was open for 9% -> 0% of each run, Pallas kernels for 0% -> 0%
where the time goes in v1:
time: 31.8 us; the launch traced here: 31.7 us
  Pallas kernels  26.5 us (83%)
  local copies, waits for them, and re-layouts  4.49 us (14%)
  between operations  0.68 us (2%)
    pallas_call x1, Pallas kernels, shards(): pl.pallas_call(functools.partial(kernel, tiles, dps, scale), out_shape=(j...  26.5 us
    unnamed x7, local copies, waits for them, and re-layouts  2.28 us
    reshape x1, local copies, waits for them, and re-layouts, shards(): act = activations.reshape(batches, half, inner)  1.13 us
    reshape x1, local copies, waits for them, and re-layouts, shards(): cot = cotangent.reshape(batches, half, inner)  1.08 us

profile of v1, /device:TPU:0, one launch (start us, length us, event | category | flops | bytes accessed | tf_op | source)
XLA Modules:
  0.0 31.7 jit_solution(6905346158632379061)
XLA Ops:
  0.6 0.0 copy-start
  0.6 1.1 %reshape.21.act = bf16[2,32,2048]{2,1,0:T(8,128)(2,1)S(1)} reshape(bf16[2,32,8,256]{3,2,1,0:T(8,128)(2,1)} %param.4) | data formatting | bytes 524288 | tf_op jit(solution)/shard_map/reshape | solution.py:343
  1.8 0.0 copy-start.1
  1.8 1.1 %reshape.22.cot = bf16[2,32,2048]{2,1,0:T(8,128)(2,1)S(1)} reshape(bf16[2,32,8,256]{3,2,1,0:T(8,128)(2,1)} %param.7) | data formatting | bytes 524288 | tf_op jit(solution)/shard_map/reshape | solution.py:344
  2.9 0.0 copy-done
  2.9 0.0 copy-done.1
  2.9 26.5 %shard_map.67 = (bf16[2,32,2048]{2,1,0:T(8,128)(2,1)S(1)}, bf16[2,32,2048]{2,1,0:T(8,128)(2,1)S(1)}, f32[27,32,64]{2,1,0:T(8,128)S(1)}) custom-call(bf16[2,32,2048]{2,1,0:T(8,128)(2,1)S(1)} %reshape.21.act, bf16[2,32,2048]{2,1,0:T(8,128)(2,1)S(1)} %reshape.22.cot, s32[2,1,2,2]{3,2,1,0:T(2,128)S(1)} %copy-done.1, bf16[27,2,32,64]{3,2,1,0:T(8,128)(2,1)S(1)} %bitcast.15), custom_call_target="tpu_custom_call" | custom-call | flops 1400000000 | bytes 2000000 | tf_op jit(solution)/shard_map/pallas_call | solution.py:347
  29.4 0.8 %copy.7 = bf16[8,8,8,256]{3,2,1,0:T(8,128)(2,1)} copy(bf16[8,8,8,256]{3,1,2,0:T(8,128)(2,1)S(1)} %bitcast.14) | data formatting | bytes 524288
  30.2 0.8 %copy.8 = bf16[8,8,8,256]{3,2,1,0:T(8,128)(2,1)} copy(bf16[8,8,8,256]{3,1,2,0:T(8,128)(2,1)S(1)} %bitcast.13) | data formatting | bytes 524288
  30.9 0.8 %copy.10 = f32[27,32,64]{2,1,0:T(8,128)} copy(f32[27,32,64]{2,1,0:T(8,128)S(1)} %get-tuple-element.14) | data formatting | bytes 442368
Async XLA Ops:
  0.6 2.2 %copy-start = (bf16[27,64,64]{2,1,0:T(8,128)(2,1)S(1)}, bf16[27,64,64]{2,1,0:T(8,128)(2,1)}, u32[]{:S(2)}) copy-start(bf16[27,64,64]{2,1,0:T(8,128)(2,1)} %param.6) | copy-start | bytes 663556
  1.8 1.1 %copy-start.1 = (s32[2,1,2,2]{3,2,1,0:T(2,128)S(1)}, s32[2,1,2,2]{3,2,1,0:T(2,128)}, u32[]{:S(2)}) copy-start(s32[2,1,2,2]{3,2,1,0:T(2,128)} %occ.1) | copy-start | bytes 100

commit v2 on v1

--- a/solution.py
+++ b/solution.py
@@ -17,7 +17,8 @@
 BF16 = jnp.bfloat16
 F32 = jnp.float32
 ROWS = 16
-TILES = 27
+REACH = 32000.0
+TINY = 1e-30
 
 
 def dot(a, b):
@@ -28,18 +29,41 @@
     return lax.dot_general(a, b, (((1,), (1,)), ((), ())), preferred_element_type=F32)
 
 
+def grades(value):
+    top = jnp.max(jnp.abs(value), axis=0, keepdims=True)
+    return jnp.ceil(jnp.log2(jnp.maximum(top, TINY)))
+
+
+def code(value, grade, data):
+    whole = jnp.round(value * (jnp.exp2(-grade) * REACH)).astype(jnp.int32)
+    rows = lax.broadcasted_iota(jnp.int32, value.shape, 0)
+    return jnp.where(rows == data, grade.astype(jnp.int32), whole).astype(jnp.int16)
+
+
+def decode(coded, data):
+    wide = coded.astype(jnp.int32).astype(F32)
+    rows = lax.broadcasted_iota(jnp.int32, wide.shape, 0)
+    grade = jnp.max(jnp.where(rows == data, wide, -REACH), axis=0, keepdims=True)
+    return jnp.where(rows < data, wide, 0.0) * (jnp.exp2(grade) * (1.0 / REACH))
+
+
 def lanes(rows):
     return lax.broadcasted_iota(jnp.int32, (rows, PLANE), 1)
 
 
 def kernel(
-    tiles, dps, scale,
-    act, cot, occ, w, out, grad_in, wg,
-    x, xe, g, ge, gd, wf, wb, part, landed, total,
-    xs, xr, gs, gr, rs, rr, ts, tr,
+    tiles, dps, scale, data,
+    act_far, cot_far, occ, w_far, out_far, grad_far, wg_far,
+    act, cot, w, out, grad_in, wg, cots, outs, x, xe, g, ge, gd, wf, wb, flat, part, landed, total,
+    near, xs, xr, gs, gr, rs, rr, ts, tr,
 ):
-    batches, half, inner = act.shape
-    depth = inner // PLANE
+    batches, half, depth, _ = act.shape
+    fetch_act = pltpu.make_async_copy(act_far, act, near.at[0])
+    fetch_w = pltpu.make_async_copy(w_far, w, near.at[1])
+    fetch_cot = pltpu.make_async_copy(cot_far, cot, near.at[2])
+    fetch_act.start()
+    fetch_w.start()
+    fetch_cot.start()
     me = {name: lax.axis_index(name) for name in ("tile", "dp", "chan")}
     t, c = me["tile"], me["chan"]
     other = 1 - c
@@ -177,15 +201,17 @@
 
     rim_zero(x)
     rim_zero(g)
-    for b in range(batches):
-        mask = live[b].astype(BF16)
-        for z in range(depth):
-            x[b, z + 1, c] = act[b, :, z * PLANE:(z + 1) * PLANE] * mask
+    fetch_act.wait()
+    for b in range(batches):
+        planes = jnp.swapaxes(act[b].astype(F32), 0, 1)
+        for z in range(depth):
+            x[b, z + 1, c] = (planes[z] * live[b]).astype(BF16)
 
     pl.semaphore_wait(barrier, count + has_up.astype(jnp.int32) + has_down.astype(jnp.int32))
     for b in range(batches):
         send_all(x, b, xs, xr)
 
+    fetch_w.wait()
     for d in range(3):
         wf[d * half:(d + 1) * half] = jnp.concatenate(
             [w[9 * a + 3 * d + e, c] for a in range(3) for e in range(3)], axis=1
@@ -208,29 +234,29 @@
     for b in range(batches):
         for z in range(depth):
             spread(xe, b, z + 1, c, x[b, z + 1, c], False)
+    fetch_cot.wait()
+    for b in range(batches):
+        cots[b] = jnp.swapaxes(cot[b].astype(F32), 0, 1)
 
     for b in range(batches):
         fill_rest(x, xe, b, xs, xr, False)
         for z in range(depth):
             pre = conv(xe, wf, b, z)
             s = 1.0 / (1.0 + jnp.exp(-pre))
-            span = slice(z * PLANE, (z + 1) * PLANE)
-            out[b, :, span] = (live[b] * (x[b, z + 1, c].astype(F32) + pre * s)).astype(BF16)
+            outs[b, z] = live[b] * (x[b, z + 1, c].astype(F32) + pre * s)
             slope = s * (1.0 + pre * (1.0 - s))
-            own = (cot[b, :, span].astype(F32) * live[b] * slope).astype(BF16)
+            own = (cots[b, z] * live[b] * slope).astype(BF16)
             g[b, z + 1, c] = own
-        send_all(g, b, gs, gr)
-        for z in range(depth):
-            own = g[b, z + 1, c]
-            spread(ge, b, z + 1, c, own, True)
-            own = own.astype(F32)
+        if b == 0:
+            send_all(g, b, gs, gr)
+        for z in range(depth):
+            own = g[b, z + 1, c].astype(F32)
             gd[b, z, 0] = jnp.where(has_below, pltpu.roll(own, PLANE - WY, 1), 0.0).astype(BF16)
             gd[b, z, 1] = g[b, z + 1, c]
             gd[b, z, 2] = jnp.where(has_above, pltpu.roll(own, WY, 1), 0.0).astype(BF16)
 
-    per = part.shape[1] // ROWS
-    for i in range(TILES, per * count):
-        part[i // per, (i % per) * ROWS:(i % per + 1) * ROWS] = jnp.zeros((ROWS, 128), F32)
+    fold = 9 * half // 2
+    flat[3 * fold:] = jnp.zeros((flat.shape[0] - 3 * fold, 128), F32)
     for a in range(3):
         acc = None
         for b in range(batches):
@@ -244,12 +270,12 @@
         body = acc[:, :4 * half]
         rest = acc[:, 4 * half:]
         mid = 3 * half // 2
-        body = jnp.concatenate(
-            [body, jnp.concatenate([rest[:mid], rest[mid:]], axis=1)], axis=0
-        )
-        for h in range(9):
-            i = 9 * a + h
-            part[i // per, (i % per) * ROWS:(i % per + 1) * ROWS] = body[h * ROWS:(h + 1) * ROWS]
+        flat[a * fold:a * fold + 3 * half] = body
+        flat[a * fold + 3 * half:(a + 1) * fold] = jnp.concatenate([rest[:mid], rest[mid:]], axis=1)
+    rows = part.shape[1]
+    grade = grades(flat[:3 * fold])
+    for i in range(count):
+        part[i] = code(flat[i * data:i * data + rows], grade, data)
 
     def scatter(j):
         r, device = member(j)
@@ -284,13 +310,21 @@
         scatter(j).start()
 
     landed[rank] = part[rank]
+    for b in range(1, batches):
+        send_all(g, b, gs, gr)
+    for b in range(batches):
+        for z in range(depth):
+            spread(ge, b, z + 1, c, g[b, z + 1, c], True)
+        out[b] = jnp.swapaxes(outs[b], 0, 1).astype(BF16)
+    leave_out = pltpu.make_async_copy(out, out_far, near.at[3])
+    leave_out.start()
 
     def backward(b):
         fill_rest(g, ge, b, gs, gr, True)
         for z in range(depth):
             back = conv(ge, wb, b, z)
-            span = slice(z * PLANE, (z + 1) * PLANE)
-            grad_in[b, :, span] = (live[b] * (cot[b, :, span].astype(F32) + back)).astype(BF16)
+            outs[b, z] = live[b] * (cots[b, z] + back)
+        grad_in[b] = jnp.swapaxes(outs[b], 0, 1).astype(BF16)
 
     backward(0)
 
@@ -298,10 +332,10 @@
     def _(j):
         scattered(j).wait_recv()
 
-    summed = landed[0]
+    summed = decode(landed[0], data)
     for i in range(1, count):
-        summed = summed + landed[i]
-    total[rank] = (summed * scale).astype(BF16)
+        summed = summed + decode(landed[i], data)
+    total[rank] = code(summed, grades(summed), data)
 
     @pl.loop(1, count)
     def _(j):
@@ -309,6 +343,8 @@
 
     for b in range(1, batches):
         backward(b)
+    leave_grad = pltpu.make_async_copy(grad_in, grad_far, near.at[4])
+    leave_grad.start()
 
     for b in range(batches):
         sent_all(x, b, xs, xr)
@@ -320,40 +356,70 @@
         gather(j).wait_send()
         gathered(j).wait_recv()
 
-    def tile(i):
-        return total[i // per, (i % per) * ROWS:(i % per + 1) * ROWS].astype(F32)
+    for i in range(count):
+        flat[i * data:(i + 1) * data] = decode(total[i], data)[:data] * scale
 
     for a in range(3):
         for h in range(6):
             d, low = h // 2, (h % 2) * ROWS
-            two = tile(9 * a + h)
-            one = tile(9 * a + 6 + h % 3)
+            start = a * fold + h * ROWS
+            two = flat[start:start + ROWS]
+            start = a * fold + 3 * half + (h % 3) * ROWS
+            one = flat[start:start + ROWS]
             k = 9 * a + 3 * d
             wg[k, low:low + ROWS] = two[:, :2 * half]
             wg[k + 1, low:low + ROWS] = two[:, 2 * half:]
             wg[k + 2, low:low + ROWS] = one[:, (h // 3) * 2 * half:(h // 3 + 1) * 2 * half]
+    leave_wg = pltpu.make_async_copy(wg, wg_far, near.at[5])
+    leave_wg.start()
+    leave_out.wait()
+    leave_grad.wait()
+    leave_wg.wait()
+
+
+def finish(a, b, c, a_out, b_out, c_out, a_mid, b_mid, c_mid, sems):
+    loads, stores = [], []
+    for i, (src, mid, dst) in enumerate(((a, a_mid, a_out), (b, b_mid, b_out), (c, c_mid, c_out))):
+        loads.append(pltpu.make_async_copy(src, mid, sems.at[0, i]))
+        stores.append(pltpu.make_async_copy(mid, dst, sems.at[1, i]))
+    for load in loads:
+        load.start()
+    for load, store in zip(loads, stores):
+        load.wait()
+        store.start()
+    for store in stores:
+        store.wait()
 
 
 def shards(tiles, dps, activations, occupancy, weight, cotangent):
     batches, half, depth, plane = activations.shape
-    inner = depth * plane
     count = tiles * dps
-    per = -(-TILES // count)
+    folded = 27 * half * 2 * half // 128
+    data = -(-folded // count)
+    rows = -(-(data + 1) // ROWS) * ROWS
     scale = 1.0 / math.sqrt(batches * dps * depth * tiles * plane)
-    act = activations.reshape(batches, half, inner)
-    cot = cotangent.reshape(batches, half, inner)
     w = weight.reshape(27, 2, half, 2 * half)
     vmem = pl.BlockSpec(memory_space=pltpu.VMEM)
-    out, grad_in, wg = pl.pallas_call(
-        functools.partial(kernel, tiles, dps, scale),
+    far = pl.BlockSpec(memory_space=pltpu.HBM)
+    full = (batches, half, depth, plane)
+    results = pl.pallas_call(
+        functools.partial(kernel, tiles, dps, scale, data),
         out_shape=(
-            jax.ShapeDtypeStruct((batches, half, inner), BF16),
-            jax.ShapeDtypeStruct((batches, half, inner), BF16),
+            jax.ShapeDtypeStruct(full, BF16),
+            jax.ShapeDtypeStruct(full, BF16),
             jax.ShapeDtypeStruct((27, half, 2 * half), F32),
         ),
-        in_specs=[vmem, vmem, pl.BlockSpec(memory_space=pltpu.SMEM), vmem],
-        out_specs=(vmem, vmem, vmem),
+        in_specs=[far, far, pl.BlockSpec(memory_space=pltpu.SMEM), far],
+        out_specs=(far, far, far),
         scratch_shapes=[
+            pltpu.VMEM(full, BF16),
+            pltpu.VMEM(full, BF16),
+            pltpu.VMEM(w.shape, BF16),
+            pltpu.VMEM(full, BF16),
+            pltpu.VMEM(full, BF16),
+            pltpu.VMEM((27, half, 2 * half), F32),
+            pltpu.VMEM((batches, depth, half, plane), F32),
+            pltpu.VMEM((batches, depth, half, plane), F32),
             pltpu.VMEM((batches, depth + 2, 2, half, plane), BF16),
             pltpu.VMEM((batches, 3 * (depth + 2), 2, half, plane), BF16),
             pltpu.VMEM((batches, depth + 2, 2, half, plane), BF16),
@@ -361,9 +427,11 @@
             pltpu.VMEM((batches, depth, 3, half, plane), BF16),
             pltpu.VMEM((3 * half, 18 * half), BF16),
             pltpu.VMEM((3 * half, 18 * half), BF16),
-            pltpu.VMEM((count, per * ROWS, 128), F32),
-            pltpu.VMEM((count, per * ROWS, 128), F32),
-            pltpu.VMEM((count, per * ROWS, 128), BF16),
+            pltpu.VMEM(((count - 1) * data + rows, 128), F32),
+            pltpu.VMEM((count, rows, 128), jnp.int16),
+            pltpu.VMEM((count, rows, 128), jnp.int16),
+            pltpu.VMEM((count, rows, 128), jnp.int16),
+            pltpu.SemaphoreType.DMA((6,)),
             pltpu.SemaphoreType.DMA((batches, 5)),
             pltpu.SemaphoreType.DMA((batches, 5)),
             pltpu.SemaphoreType.DMA((batches, 5)),
@@ -374,12 +442,18 @@
             pltpu.SemaphoreType.DMA((count,)),
         ],
         compiler_params=pltpu.CompilerParams(
-            collective_id=0, has_side_effects=True, vmem_limit_bytes=40 * 1024 * 1024
+            collective_id=0, has_side_effects=True, vmem_limit_bytes=60 * 1024 * 1024
         ),
         cost_estimate=pl.CostEstimate(flops=1400000000, bytes_accessed=2000000, transcendentals=131072),
-    )(act, cot, occupancy, w)
-    shape = (batches, half, depth, plane)
-    return out.reshape(shape), grad_in.reshape(shape), wg
+    )(activations, cotangent, occupancy, w)
+    return pl.pallas_call(
+        finish,
+        out_shape=tuple(jax.ShapeDtypeStruct(r.shape, r.dtype) for r in results),
+        in_specs=[far, far, far],
+        out_specs=(far, far, far),
+        scratch_shapes=[pltpu.VMEM(r.shape, r.dtype) for r in results] + [pltpu.SemaphoreType.DMA((2, 3))],
+        compiler_params=pltpu.CompilerParams(vmem_limit_bytes=60 * 1024 * 1024),
+    )(*results)
 
 
 def solution(mesh):

time: 31.8 us -> 27.5 us (0.86)
  local copies, waits for them, and re-layouts: 4.49 us -> 0 us
    unnamed x7 -> x0, local copies, waits for them, and re-layouts: 2.28 us -> none
    reshape x2 -> x0, local copies, waits for them, and re-layouts: 2.21 us -> none  [the longest x1 1.13 us: shards(): act = activations.reshape(batches, half, inner)]
    pallas_call x1 -> x2, Pallas kernels: 26.5 us -> 26.7 us  [the longest x1 24.7 us: shards(): pl.pallas_call(functools.partial(kernel, tiles, dps, scale, data), out_sh...]
where the time goes in v2:
time: 27.5 us; the launch traced here: 27.3 us
  Pallas kernels  26.7 us (97%)
  between operations  0.64 us (2%)
    pallas_call x1, Pallas kernels, shards(): pl.pallas_call(functools.partial(kernel, tiles, dps, scale, data), out_sh...  24.7 us
    pallas_call x1, Pallas kernels, shards(): pl.pallas_call(finish, out_shape=tuple((jax.ShapeDtypeStruct(r.shape, r.d...  1.99 us

profile of v2, /device:TPU:0, one launch (start us, length us, event | category | flops | bytes accessed | tf_op | source)
XLA Modules:
  0.0 27.3 jit_solution(14025351427601944689)
XLA Ops:
  0.6 24.7 %shard_map.67 = (bf16[2,32,8,256]{3,2,1,0:T(8,128)(2,1)}, bf16[2,32,8,256]{3,2,1,0:T(8,128)(2,1)}, f32[27,32,64]{2,1,0:T(8,128)}) custom-call(bf16[2,32,8,256]{3,2,1,0:T(8,128)(2,1)} %act_far.1, bf16[2,32,8,256]{3,2,1,0:T(8,128)(2,1)} %cot_far.1, s32[2,1,2,2]{3,2,1,0:T(2,128)} %occ.1, bf16[27,2,32,64]{3,2,1,0:T(8,128)(2,1)} %bitcast.1), custom_call_target="tpu_custom_call" | custom-call | flops 1400000000 | bytes 2000000 | tf_op jit(solution)/shard_map/pallas_call | solution.py:405
  25.3 2.0 %shard_map.68 = (bf16[2,32,8,256]{3,2,1,0:T(8,128)(2,1)}, bf16[2,32,8,256]{3,2,1,0:T(8,128)(2,1)}, f32[27,32,64]{2,1,0:T(8,128)}) custom-call(bf16[2,32,8,256]{3,2,1,0:T(8,128)(2,1)} %get-tuple-element.6.a, bf16[2,32,8,256]{3,2,1,0:T(8,128)(2,1)} %get-tuple-element.7.b, f32[27,32,64]{2,1,0:T(8,128)} %get-tuple-element.8.c), custom_call_target="tpu_custom_call" | custom-call | tf_op jit(solution)/shard_map/pallas_call | solution.py:449

commit v3 on v2

--- a/solution.py
+++ b/solution.py
@@ -52,9 +52,9 @@
 
 
 def kernel(
-    tiles, dps, scale, data,
-    act_far, cot_far, occ, w_far, out_far, grad_far, wg_far,
-    act, cot, w, out, grad_in, wg, cots, outs, x, xe, g, ge, gd, wf, wb, flat, part, landed, total,
+    tiles, dps, data,
+    act_far, cot_far, occ, w_far, out_far, grad_far, total_far,
+    act, cot, w, out, grad_in, cots, outs, x, xe, g, ge, gd, wf, wb, flat, part, landed, total,
     near, xs, xr, gs, gr, rs, rr, ts, tr,
 ):
     batches, half, depth, _ = act.shape
@@ -184,10 +184,12 @@
             for ch in range(2):
                 rim(buf, b, ch, False, 0, send, recv).wait_recv()
 
-    def fill_rest(buf, dst, b, send, recv, flip):
+    def fill_inner(buf, dst, b, send, recv, flip):
         inside(buf, b, other, send, recv).wait_recv()
         for z in range(depth):
             spread(dst, b, z + 1, other, buf[b, z + 1, other], flip)
+
+    def fill_rims(buf, dst, b, send, recv, flip):
         rims_arrive(buf, b, send, recv)
         for q in (0, depth + 1):
             for ch in range(2):
@@ -238,22 +240,28 @@
     for b in range(batches):
         cots[b] = jnp.swapaxes(cot[b].astype(F32), 0, 1)
 
-    for b in range(batches):
-        fill_rest(x, xe, b, xs, xr, False)
-        for z in range(depth):
-            pre = conv(xe, wf, b, z)
-            s = 1.0 / (1.0 + jnp.exp(-pre))
-            outs[b, z] = live[b] * (x[b, z + 1, c].astype(F32) + pre * s)
-            slope = s * (1.0 + pre * (1.0 - s))
-            own = (cots[b, z] * live[b] * slope).astype(BF16)
-            g[b, z + 1, c] = own
+    def forward(b, z):
+        pre = conv(xe, wf, b, z)
+        s = 1.0 / (1.0 + jnp.exp(-pre))
+        outs[b, z] = live[b] * (x[b, z + 1, c].astype(F32) + pre * s)
+        slope = s * (1.0 + pre * (1.0 - s))
+        own = (cots[b, z] * live[b] * slope).astype(BF16)
+        g[b, z + 1, c] = own
+        wide = own.astype(F32)
+        gd[b, z, 0] = jnp.where(has_below, pltpu.roll(wide, PLANE - WY, 1), 0.0).astype(BF16)
+        gd[b, z, 1] = own
+        gd[b, z, 2] = jnp.where(has_above, pltpu.roll(wide, WY, 1), 0.0).astype(BF16)
+
+    for b in range(batches):
+        fill_inner(x, xe, b, xs, xr, False)
+        for z in range(1, depth - 1):
+            forward(b, z)
+    for b in range(batches):
+        fill_rims(x, xe, b, xs, xr, False)
+        for z in (0, depth - 1):
+            forward(b, z)
         if b == 0:
             send_all(g, b, gs, gr)
-        for z in range(depth):
-            own = g[b, z + 1, c].astype(F32)
-            gd[b, z, 0] = jnp.where(has_below, pltpu.roll(own, PLANE - WY, 1), 0.0).astype(BF16)
-            gd[b, z, 1] = g[b, z + 1, c]
-            gd[b, z, 2] = jnp.where(has_above, pltpu.roll(own, WY, 1), 0.0).astype(BF16)
 
     fold = 9 * half // 2
     flat[3 * fold:] = jnp.zeros((flat.shape[0] - 3 * fold, 128), F32)
@@ -320,7 +328,8 @@
     leave_out.start()
 
     def backward(b):
-        fill_rest(g, ge, b, gs, gr, True)
+        fill_inner(g, ge, b, gs, gr, True)
+        fill_rims(g, ge, b, gs, gr, True)
         for z in range(depth):
             back = conv(ge, wb, b, z)
             outs[b, z] = live[b] * (cots[b, z] + back)
@@ -346,6 +355,12 @@
     leave_grad = pltpu.make_async_copy(grad_in, grad_far, near.at[4])
     leave_grad.start()
 
+    @pl.loop(1, count)
+    def _(j):
+        gathered(j).wait_recv()
+
+    leave_total = pltpu.make_async_copy(total, total_far, near.at[5])
+    leave_total.start()
     for b in range(batches):
         sent_all(x, b, xs, xr)
         sent_all(g, b, gs, gr)
@@ -354,8 +369,27 @@
     def _(j):
         scatter(j).wait_send()
         gather(j).wait_send()
-        gathered(j).wait_recv()
-
+
+    leave_out.wait()
+    leave_grad.wait()
+    leave_total.wait()
+
+
+def finish(scale, data, a, b, c, a_out, b_out, wg_out, a_mid, b_mid, total, flat, wg, sems):
+    loads = [
+        pltpu.make_async_copy(src, mid, sems.at[0, i])
+        for i, (src, mid) in enumerate(((c, total), (a, a_mid), (b, b_mid)))
+    ]
+    stores = [
+        pltpu.make_async_copy(mid, dst, sems.at[1, i])
+        for i, (mid, dst) in enumerate(((wg, wg_out), (a_mid, a_out), (b_mid, b_out)))
+    ]
+    for load in loads:
+        load.start()
+    loads[0].wait()
+    count = total.shape[0]
+    half = wg.shape[1]
+    fold = 9 * half // 2
     for i in range(count):
         flat[i * data:(i + 1) * data] = decode(total[i], data)[:data] * scale
 
@@ -370,21 +404,8 @@
             wg[k, low:low + ROWS] = two[:, :2 * half]
             wg[k + 1, low:low + ROWS] = two[:, 2 * half:]
             wg[k + 2, low:low + ROWS] = one[:, (h // 3) * 2 * half:(h // 3 + 1) * 2 * half]
-    leave_wg = pltpu.make_async_copy(wg, wg_far, near.at[5])
-    leave_wg.start()
-    leave_out.wait()
-    leave_grad.wait()
-    leave_wg.wait()
-
-
-def finish(a, b, c, a_out, b_out, c_out, a_mid, b_mid, c_mid, sems):
-    loads, stores = [], []
-    for i, (src, mid, dst) in enumerate(((a, a_mid, a_out), (b, b_mid, b_out), (c, c_mid, c_out))):
-        loads.append(pltpu.make_async_copy(src, mid, sems.at[0, i]))
-        stores.append(pltpu.make_async_copy(mid, dst, sems.at[1, i]))
-    for load in loads:
-        load.start()
-    for load, store in zip(loads, stores):
+    stores[0].start()
+    for load, store in zip(loads[1:], stores[1:]):
         load.wait()
         store.start()
     for store in stores:
@@ -403,11 +424,11 @@
     far = pl.BlockSpec(memory_space=pltpu.HBM)
     full = (batches, half, depth, plane)
     results = pl.pallas_call(
-        functools.partial(kernel, tiles, dps, scale, data),
+        functools.partial(kernel, tiles, dps, data),
         out_shape=(
             jax.ShapeDtypeStruct(full, BF16),
             jax.ShapeDtypeStruct(full, BF16),
-            jax.ShapeDtypeStruct((27, half, 2 * half), F32),
+            jax.ShapeDtypeStruct((count, rows, 128), jnp.int16),
         ),
         in_specs=[far, far, pl.BlockSpec(memory_space=pltpu.SMEM), far],
         out_specs=(far, far, far),
@@ -417,7 +438,6 @@
             pltpu.VMEM(w.shape, BF16),
             pltpu.VMEM(full, BF16),
             pltpu.VMEM(full, BF16),
-            pltpu.VMEM((27, half, 2 * half), F32),
             pltpu.VMEM((batches, depth, half, plane), F32),
             pltpu.VMEM((batches, depth, half, plane), F32),
             pltpu.VMEM((batches, depth + 2, 2, half, plane), BF16),
@@ -447,11 +467,22 @@
         cost_estimate=pl.CostEstimate(flops=1400000000, bytes_accessed=2000000, transcendentals=131072),
     )(activations, cotangent, occupancy, w)
     return pl.pallas_call(
-        finish,
-        out_shape=tuple(jax.ShapeDtypeStruct(r.shape, r.dtype) for r in results),
+        functools.partial(finish, scale, data),
+        out_shape=(
+            jax.ShapeDtypeStruct(full, BF16),
+            jax.ShapeDtypeStruct(full, BF16),
+            jax.ShapeDtypeStruct((27, half, 2 * half), F32),
+        ),
         in_specs=[far, far, far],
         out_specs=(far, far, far),
-        scratch_shapes=[pltpu.VMEM(r.shape, r.dtype) for r in results] + [pltpu.SemaphoreType.DMA((2, 3))],
+        scratch_shapes=[
+            pltpu.VMEM(full, BF16),
+            pltpu.VMEM(full, BF16),
+            pltpu.VMEM((count, rows, 128), jnp.int16),
+            pltpu.VMEM((count * data, 128), F32),
+            pltpu.VMEM((27, half, 2 * half), F32),
+            pltpu.SemaphoreType.DMA((2, 3)),
+        ],
         compiler_params=pltpu.CompilerParams(vmem_limit_bytes=60 * 1024 * 1024),
     )(*results)
 

time: 27.5 us -> 26.7 us (0.971)
  Pallas kernels: 26.7 us -> 25.9 us
    pallas_call x2, Pallas kernels: 26.7 us -> 25.9 us  [the longest x1 23.8 us: shards(): pl.pallas_call(functools.partial(kernel, tiles, dps, data), out_shape=(ja...]
where the time goes in v3:
time: 26.7 us; the launch traced here: 26.5 us
  Pallas kernels  25.9 us (97%)
  between operations  0.64 us (2%)
    pallas_call x1, Pallas kernels, shards(): pl.pallas_call(functools.partial(kernel, tiles, dps, data), out_shape=(ja...  23.8 us
    pallas_call x1, Pallas kernels, shards(): pl.pallas_call(functools.partial(finish, scale, data), out_shape=(jax.Sha...  2.05 us

profile of v3, /device:TPU:0, one launch (start us, length us, event | category | flops | bytes accessed | tf_op | source)
XLA Modules:
  0.0 26.5 jit_solution(17361042012298518301)
XLA Ops:
  0.6 23.8 %shard_map.67 = (bf16[2,32,8,256]{3,2,1,0:T(8,128)(2,1)}, bf16[2,32,8,256]{3,2,1,0:T(8,128)(2,1)}, s16[8,64,128]{2,1,0:T(8,128)(2,1)}) custom-call(bf16[2,32,8,256]{3,2,1,0:T(8,128)(2,1)} %act_far.1, bf16[2,32,8,256]{3,2,1,0:T(8,128)(2,1)} %cot_far.1, s32[2,1,2,2]{3,2,1,0:T(2,128)} %occ.1, bf16[27,2,32,64]{3,2,1,0:T(8,128)(2,1)} %bitcast.1), custom_call_target="tpu_custom_call" | custom-call | flops 1400000000 | bytes 2000000 | tf_op jit(solution)/shard_map/pallas_call | solution.py:426
  24.5 2.0 %shard_map.68 = (bf16[2,32,8,256]{3,2,1,0:T(8,128)(2,1)}, bf16[2,32,8,256]{3,2,1,0:T(8,128)(2,1)}, f32[27,32,64]{2,1,0:T(8,128)}) custom-call(bf16[2,32,8,256]{3,2,1,0:T(8,128)(2,1)} %get-tuple-element.6.a, bf16[2,32,8,256]{3,2,1,0:T(8,128)(2,1)} %get-tuple-element.7.b, s16[8,64,128]{2,1,0:T(8,128)(2,1)} %get-tuple-element.8.c), custom_call_target="tpu_custom_call" | custom-call | tf_op jit(solution)/shard_map/pallas_call | solution.py:469
